TPU v7x, 32 devices: a whole 2x2x4 slice. The times are simulated.
32 devices in a mesh: chan: 8 (over z, core), hour: 4 (over y, x).
Axes of the slice: x: 2, y: 2, z: 4, core: 2. Of those that a mesh axis runs over, the one named last changes fastest.
Arguments:
- spectra: bfloat16 [32, 64, 4096], P('hour', 'chan'), may hold values from -200 to 200
- quality: int32 [64], P('chan'), may hold values 0 or 1
- plan: int32 [4], replicated, may hold values from 1 to 7, as said below
Outputs:
- correlations: float32 [4, 8, 64, 512], P(None, 'hour', 'chan')
Inputs may be any that keep to these rules, and one draw needn't show every extreme that they name: `plan`: distinct numbers; 1 and 7 are among them.
All inputs are finite; a program needn't handle non-finite values. No bound on the sum of `quality` on one device may be relied on, other than what follows from the above.
Results may differ from a plain program's by a relative error of at most 0.004.
Values may be sent and summed in bfloat16 or wider, within the bound.
A program may use at most 320 MiB of HBM per device.

v0:
```python
import jax
import jax.numpy as jnp
from jax import lax
from jax.sharding import PartitionSpec as P

BAND = 64
LAGS = 512
ROUNDS = 4


def partner_2(value, axis, apart):
    return lax.ppermute(value, axis, [(i, i ^ 1 << apart) for i in range(lax.axis_size(axis))])


def whiten(spectra, quality):
    hours, chans, width = spectra.shape
    n_freq = width // 2
    values = spectra.astype(jnp.float32)
    real_part = values[..., :n_freq]
    imag_part = values[..., n_freq:]
    power_sum = real_part * real_part + imag_part * imag_part
    band_mean = jnp.mean(
        power_sum.reshape(hours, chans, n_freq // BAND, BAND), axis=-1, keepdims=True
    )
    gain_band = lax.rsqrt(band_mean + 1e-06)
    gain_full = jnp.broadcast_to(gain_band, (hours, chans, n_freq // BAND, BAND)).reshape(
        hours, chans, n_freq
    )
    gain_both = jnp.concatenate([gain_full, gain_full], axis=-1)
    scaled = values * gain_both * quality.astype(jnp.float32)[None, :, None]
    return scaled.astype(jnp.bfloat16)


def lag_table(n_freq, total_hours):
    freq_index = jnp.arange(n_freq, dtype=jnp.int32)[:, None]
    lag_index = jnp.arange(LAGS, dtype=jnp.int32)[None, :] - LAGS // 2
    phase_int = freq_index * lag_index % (2 * n_freq)
    angle = jnp.pi * phase_int.astype(jnp.float32) / n_freq
    factor = 1.0 / jnp.sqrt(jnp.float32(total_hours * n_freq))
    return jnp.concatenate([jnp.cos(angle), -jnp.sin(angle)], axis=0) * factor


def cross_spectrum(own_block, partner):
    n_freq = own_block.shape[2] // 2
    own_re = own_block[..., :n_freq]
    own_im = own_block[..., n_freq:]
    far_re = partner[..., :n_freq]
    far_im = partner[..., n_freq:]
    f32 = jnp.float32
    cross_re = jnp.einsum("hjf,hif->jif", far_re, own_re, preferred_element_type=f32) + jnp.einsum(
        "hjf,hif->jif", far_im, own_im, preferred_element_type=f32
    )
    cross_im = jnp.einsum("hjf,hif->jif", far_re, own_im, preferred_element_type=f32) - jnp.einsum(
        "hjf,hif->jif", far_im, own_re, preferred_element_type=f32
    )
    return jnp.concatenate([cross_re, cross_im], axis=-1)


def to_lags(cross_spec, weights):
    rows_far, rows_own, width = cross_spec.shape
    flat = cross_spec.reshape(rows_far * rows_own, width)
    lagged = jnp.dot(
        flat, weights, precision=lax.Precision.HIGHEST, preferred_element_type=jnp.float32
    )
    return lagged.reshape(rows_far, rows_own, weights.shape[1])


def per_device(spectra, quality, plan):
    hours, chans, width = spectra.shape
    n_freq = width // 2
    own_block = whiten(spectra, quality)
    weights = lag_table(n_freq, hours * lax.axis_size("hour"))
    bit_count = lax.axis_size("chan").bit_length() - 1
    results = []
    for rnd_index in range(ROUNDS):
        xor_mask = plan[rnd_index]
        partner = own_block
        for bit_pos in range(bit_count):
            moved = partner_2(partner, "chan", bit_pos)
            partner = jnp.where(
                jnp.bitwise_and(jnp.right_shift(xor_mask, bit_pos), 1) == 1, moved, partner
            )

        def term_rows(start, count, partner=partner):
            return to_lags(cross_spectrum(own_block, partner), weights)

        stacked = lax.psum_scatter(
            term_rows(jnp.int32(0), lax.axis_size("hour") * (chans // lax.axis_size("hour"))),
            "hour",
            scatter_dimension=0,
            tiled=True,
        )
        results.append(stacked)
    return jnp.stack(results)


def solution(mesh):
    return jax.shard_map(
        per_device,
        mesh=mesh,
        in_specs=(P("hour", "chan", None), P("chan"), P()),
        out_specs=P(None, "hour", "chan", None),
        check_vma=False,
    )
```

profile of v0, /device:TPU:0, one launch (start us, length us, event | category | flops | bytes accessed | tf_op | source)
XLA Modules:
  0.0 425.3 jit_solution(10500795309202309557)
XLA Ops:
  18.3 4.1 copy.7
  29.2 17.9 %fusion.15 = (f32[2048,512]{1,0:T(8,128)}, f32[2048,512]{1,0:T(8,128)}) fusion(s32[512]{0:T(512)S(1)} %iota_add_fusion), kind=kLoop, calls=%fused_computation.16 | loop fusion | flops 15728640 | bytes 8390656 | tf_op jit(solution)/shard_map/cos | solution.py:40
  52.3 20.8 %collective-permute-done.3 = bf16[8,8,4096]{2,1,0:T(8,128)(2,1)S(1)} collective-permute-done((bf16[8,8,4096]{2,1,0:T(8,128)(2,1)S(1)}, bf16[8,8,4096]{2,1,0:T(8,128)(2,1)S(1)}, u32[]{:S(2)}, u32[]{:S(2)}) %collective-permute-start.3) | collective-permute-done | bytes 524320 | tf_op jit(solution)/shard_map/ppermute | solution.py:12
  73.8 20.9 %collective-permute-done.5 = bf16[8,8,4096]{2,1,0:T(8,128)(2,1)S(1)} collective-permute-done((bf16[8,8,4096]{2,1,0:T(8,128)(2,1)S(1)}, bf16[8,8,4096]{2,1,0:T(8,128)(2,1)S(1)}, u32[]{:S(2)}, u32[]{:S(2)}) %collective-permute-start.5) | collective-permute-done | bytes 524320 | tf_op jit(solution)/shard_map/ppermute | solution.py:12
  94.8 10.4 %collective-permute-done.7 = bf16[8,8,4096]{2,1,0:T(8,128)(2,1)S(1)} collective-permute-done((bf16[8,8,4096]{2,1,0:T(8,128)(2,1)S(1)}, bf16[8,8,4096]{2,1,0:T(8,128)(2,1)S(1)}, u32[]{:S(2)}, u32[]{:S(2)}) %collective-permute-start.7) | collective-permute-done | bytes 524320 | tf_op jit(solution)/shard_map/ppermute | solution.py:12
  105.4 4.0 copy.5
  109.5 4.4 %copy.8 = bf16[8,8,2048]{1,0,2:T(8,128)(2,1)} copy(bf16[8,8,2048]{2,1,0:T(8,128)(2,1)S(1)} %get-tuple-element.9) | data formatting | bytes 524288 | tf_op jit(solution)/shard_map/slice | solution.py:48
  113.9 9.2 %fusion.47 = f32[2048,8,8]{2,1,0:T(8,128)} fusion(bf16[8,8,2048]{0,1,2:T(8,128)(2,1)} %copy.7, bf16[8,8,2048]{1,0,2:T(8,128)(2,1)} %copy.5), kind=kOutput, calls=%fused_computation.74 | convolution fusion | flops 2097152 | bytes 1048576 | tf_op jit(solution)/shard_map/hjf,hif->jif/dot_general | solution.py:53
  123.1 5.6 %fusion.45 = f32[2048,8,8]{2,1,0:T(8,128)} fusion(bf16[8,8,2048]{0,1,2:T(8,128)(2,1)S(1)} %copy-done.4, bf16[8,8,2048]{1,0,2:T(8,128)(2,1)S(1)} %copy-done.8), kind=kOutput, calls=%fused_computation.72 | convolution fusion | flops 2097152 | bytes 1048576 | tf_op jit(solution)/shard_map/hjf,hif->jif/dot_general | solution.py:50
  128.6 5.6 %fusion.48 = f32[2048,8,8]{2,1,0:T(8,128)} fusion(bf16[8,8,2048]{0,1,2:T(8,128)(2,1)S(1)} %copy-done.4, bf16[8,8,2048]{1,0,2:T(8,128)(2,1)S(1)} %copy-done.9), kind=kOutput, calls=%fused_computation.75 | convolution fusion | flops 2097152 | bytes 1048576 | tf_op jit(solution)/shard_map/hjf,hif->jif/dot_general | solution.py:53
  134.2 5.6 %fusion.46 = f32[2048,8,8]{2,1,0:T(8,128)} fusion(bf16[8,8,2048]{0,1,2:T(8,128)(2,1)S(1)} %copy-done, bf16[8,8,2048]{1,0,2:T(8,128)(2,1)S(1)} %copy-done.9), kind=kOutput, calls=%fused_computation.73 | convolution fusion | flops 2097152 | bytes 1048576 | tf_op jit(solution)/shard_map/hjf,hif->jif/dot_general | solution.py:50
  139.9 4.2 copy.12
  144.1 9.2 %fusion.49 = f32[2048,8,8]{2,1,0:T(8,128)} fusion(bf16[8,8,2048]{0,1,2:T(8,128)(2,1)} %copy.4, bf16[8,8,2048]{1,0,2:T(8,128)(2,1)} %copy.12), kind=kOutput, calls=%fused_computation.76 | convolution fusion | flops 2097152 | bytes 1048576 | tf_op jit(solution)/shard_map/hjf,hif->jif/dot_general | solution.py:50
  153.3 5.5 %fusion.51 = f32[2048,8,8]{2,1,0:T(8,128)} fusion(bf16[8,8,2048]{0,1,2:T(8,128)(2,1)S(1)} %copy-done.1, bf16[8,8,2048]{1,0,2:T(8,128)(2,1)S(1)} %copy-done.11), kind=kOutput, calls=%fused_computation.78 | convolution fusion | flops 2097152 | bytes 1048576 | tf_op jit(solution)/shard_map/hjf,hif->jif/dot_general | solution.py:53
  162.8 9.1 %fusion.50 = f32[2048,8,8]{2,1,0:T(8,128)} fusion(bf16[8,8,2048]{0,1,2:T(8,128)(2,1)} %copy.7, bf16[8,8,2048]{1,0,2:T(8,128)(2,1)} %copy.14), kind=kOutput, calls=%fused_computation.77 | convolution fusion | flops 2097152 | bytes 1048576 | tf_op jit(solution)/shard_map/hjf,hif->jif/dot_general | solution.py:50
  171.9 5.6 %fusion.52 = f32[2048,8,8]{2,1,0:T(8,128)} fusion(bf16[8,8,2048]{0,1,2:T(8,128)(2,1)S(1)} %copy-done.5, bf16[8,8,2048]{1,0,2:T(8,128)(2,1)S(1)} %copy-done.12), kind=kOutput, calls=%fused_computation.79 | convolution fusion | flops 2097152 | bytes 1048576 | tf_op jit(solution)/shard_map/hjf,hif->jif/dot_general | solution.py:53
  177.6 4.2 copy.18
  181.8 9.2 %fusion.53 = f32[2048,8,8]{2,1,0:T(8,128)} fusion(bf16[8,8,2048]{0,1,2:T(8,128)(2,1)} %copy.4, bf16[8,8,2048]{1,0,2:T(8,128)(2,1)} %copy.18), kind=kOutput, calls=%fused_computation.80 | convolution fusion | flops 2097152 | bytes 1048576 | tf_op jit(solution)/shard_map/hjf,hif->jif/dot_general | solution.py:50
  191.1 5.6 %fusion.55 = f32[2048,8,8]{2,1,0:T(8,128)} fusion(bf16[8,8,2048]{0,1,2:T(8,128)(2,1)S(1)} %copy-done.2, bf16[8,8,2048]{1,0,2:T(8,128)(2,1)S(1)} %copy-done.13), kind=kOutput, calls=%fused_computation.82 | convolution fusion | flops 2097152 | bytes 1048576 | tf_op jit(solution)/shard_map/hjf,hif->jif/dot_general | solution.py:53
  200.6 9.1 %fusion.54 = f32[2048,8,8]{2,1,0:T(8,128)} fusion(bf16[8,8,2048]{0,1,2:T(8,128)(2,1)} %copy.7, bf16[8,8,2048]{1,0,2:T(8,128)(2,1)} %copy.20), kind=kOutput, calls=%fused_computation.81 | convolution fusion | flops 2097152 | bytes 1048576 | tf_op jit(solution)/shard_map/hjf,hif->jif/dot_general | solution.py:50
  209.8 5.6 %fusion.56 = f32[2048,8,8]{2,1,0:T(8,128)} fusion(bf16[8,8,2048]{0,1,2:T(8,128)(2,1)S(1)} %copy-done.6, bf16[8,8,2048]{1,0,2:T(8,128)(2,1)S(1)} %copy-done.14), kind=kOutput, calls=%fused_computation.83 | convolution fusion | flops 2097152 | bytes 1048576 | tf_op jit(solution)/shard_map/hjf,hif->jif/dot_general | solution.py:53
  215.5 4.4 %copy.26 = bf16[8,8,2048]{1,0,2:T(8,128)(2,1)} copy(bf16[8,8,2048]{2,1,0:T(8,128)(2,1)S(1)} %get-tuple-element.15) | data formatting | bytes 524288 | tf_op jit(solution)/shard_map/slice | solution.py:48
  220.0 9.2 %fusion.58 = f32[2048,8,8]{2,1,0:T(8,128)} fusion(bf16[8,8,2048]{0,1,2:T(8,128)(2,1)} %copy.7, bf16[8,8,2048]{1,0,2:T(8,128)(2,1)} %copy.26), kind=kOutput, calls=%fused_computation.85 | convolution fusion | flops 2097152 | bytes 1048576 | tf_op jit(solution)/shard_map/hjf,hif->jif/dot_general | solution.py:50
  229.1 5.6 %fusion.60 = f32[2048,8,8]{2,1,0:T(8,128)} fusion(bf16[8,8,2048]{0,1,2:T(8,128)(2,1)S(1)} %copy-done.7, bf16[8,8,2048]{1,0,2:T(8,128)(2,1)S(1)} %copy-done.15), kind=kOutput, calls=%fused_computation.87 | convolution fusion | flops 2097152 | bytes 1048576 | tf_op jit(solution)/shard_map/hjf,hif->jif/dot_general | solution.py:53
  238.8 9.2 %fusion.57 = f32[2048,8,8]{2,1,0:T(8,128)} fusion(bf16[8,8,2048]{0,1,2:T(8,128)(2,1)} %copy.4, bf16[8,8,2048]{1,0,2:T(8,128)(2,1)} %copy.24), kind=kOutput, calls=%fused_computation.84 | convolution fusion | flops 2097152 | bytes 1048576 | tf_op jit(solution)/shard_map/hjf,hif->jif/dot_general | solution.py:50
  248.0 5.5 %fusion.59 = f32[2048,8,8]{2,1,0:T(8,128)} fusion(bf16[8,8,2048]{0,1,2:T(8,128)(2,1)S(1)} %copy-done.3, bf16[8,8,2048]{1,0,2:T(8,128)(2,1)S(1)} %copy-done.10), kind=kOutput, calls=%fused_computation.86 | convolution fusion | flops 2097152 | bytes 1048576 | tf_op jit(solution)/shard_map/hjf,hif->jif/dot_general | solution.py:53
  253.5 5.2 %copy.10 = f32[2048,8,8]{0,1,2:T(8,128)S(1)} copy(f32[2048,8,8]{2,1,0:T(8,128)} %fusion.47) | data formatting | bytes 1048576 | tf_op jit(solution)/shard_map/hjf,hif->jif/dot_general | solution.py:53
  258.7 5.2 %copy.11 = f32[2048,8,8]{0,1,2:T(8,128)S(1)} copy(f32[2048,8,8]{2,1,0:T(8,128)} %fusion.48) | data formatting | bytes 1048576 | tf_op jit(solution)/shard_map/hjf,hif->jif/dot_general | solution.py:53
  263.9 5.2 %copy.6 = f32[2048,8,8]{0,1,2:T(8,128)S(1)} copy(f32[2048,8,8]{2,1,0:T(8,128)} %fusion.45) | data formatting | bytes 1048576 | tf_op jit(solution)/shard_map/hjf,hif->jif/dot_general | solution.py:50
  269.1 5.4 %copy.9 = f32[2048,8,8]{0,1,2:T(8,128)S(1)} copy(f32[2048,8,8]{2,1,0:T(8,128)} %fusion.46) | data formatting | bytes 1048576 | tf_op jit(solution)/shard_map/hjf,hif->jif/dot_general | solution.py:50
  274.6 9.4 %fusion.13 = f32[8,8,512]{2,1,0:T(8,128)} fusion(f32[2048,512]{1,0:T(8,128)} %get-tuple-element.20, f32[2048,512]{1,0:T(8,128)} %get-tuple-element.19, f32[8,8,2048]{2,1,0:T(8,128)S(1)} %get-tuple-element.31, f32[8,8,2048]{2,1,0:T(8,128)S(1)} %get-tuple-element.32), kind=kOutput, calls=%fused_computation.15 | convolution fusion | flops 1615069184 | bytes 9568256 | tf_op jit(solution)/shard_map/dot_general | solution.py:62
  284.1 5.2 %copy.13 = f32[2048,8,8]{0,1,2:T(8,128)S(1)} copy(f32[2048,8,8]{2,1,0:T(8,128)} %fusion.49) | data formatting | bytes 1048576 | tf_op jit(solution)/shard_map/hjf,hif->jif/dot_general | solution.py:50
  289.2 5.2 %copy.15 = f32[2048,8,8]{0,1,2:T(8,128)S(1)} copy(f32[2048,8,8]{2,1,0:T(8,128)} %fusion.50) | data formatting | bytes 1048576 | tf_op jit(solution)/shard_map/hjf,hif->jif/dot_general | solution.py:50
  294.5 5.2 %copy.16 = f32[2048,8,8]{0,1,2:T(8,128)S(1)} copy(f32[2048,8,8]{2,1,0:T(8,128)} %fusion.51) | data formatting | bytes 1048576 | tf_op jit(solution)/shard_map/hjf,hif->jif/dot_general | solution.py:53
  299.7 5.2 %copy.17 = f32[2048,8,8]{0,1,2:T(8,128)S(1)} copy(f32[2048,8,8]{2,1,0:T(8,128)} %fusion.52) | data formatting | bytes 1048576 | tf_op jit(solution)/shard_map/hjf,hif->jif/dot_general | solution.py:53
  305.0 5.2 %copy.19 = f32[2048,8,8]{0,1,2:T(8,128)S(1)} copy(f32[2048,8,8]{2,1,0:T(8,128)} %fusion.53) | data formatting | bytes 1048576 | tf_op jit(solution)/shard_map/hjf,hif->jif/dot_general | solution.py:50
  310.2 5.2 %copy.21 = f32[2048,8,8]{0,1,2:T(8,128)S(1)} copy(f32[2048,8,8]{2,1,0:T(8,128)} %fusion.54) | data formatting | bytes 1048576 | tf_op jit(solution)/shard_map/hjf,hif->jif/dot_general | solution.py:50
  315.4 5.2 %copy.22 = f32[2048,8,8]{0,1,2:T(8,128)S(1)} copy(f32[2048,8,8]{2,1,0:T(8,128)} %fusion.55) | data formatting | bytes 1048576 | tf_op jit(solution)/shard_map/hjf,hif->jif/dot_general | solution.py:53
  320.6 5.2 %copy.23 = f32[2048,8,8]{0,1,2:T(8,128)S(1)} copy(f32[2048,8,8]{2,1,0:T(8,128)} %fusion.56) | data formatting | bytes 1048576 | tf_op jit(solution)/shard_map/hjf,hif->jif/dot_general | solution.py:53
  325.8 9.4 %fusion.11 = f32[8,8,512]{2,1,0:T(8,128)} fusion(f32[2048,512]{1,0:T(8,128)} %get-tuple-element.20, f32[2048,512]{1,0:T(8,128)} %get-tuple-element.19, f32[8,8,2048]{2,1,0:T(8,128)S(1)} %get-tuple-element.29, f32[8,8,2048]{2,1,0:T(8,128)S(1)} %get-tuple-element.30), kind=kOutput, calls=%fused_computation.14 | convolution fusion | flops 1615069184 | bytes 9568256 | tf_op jit(solution)/shard_map/dot_general | solution.py:62
  335.4 5.4 %copy.25 = f32[2048,8,8]{0,1,2:T(8,128)S(1)} copy(f32[2048,8,8]{2,1,0:T(8,128)} %fusion.57) | data formatting | bytes 1048576 | tf_op jit(solution)/shard_map/hjf,hif->jif/dot_general | solution.py:50
  340.8 5.2 %copy.27 = f32[2048,8,8]{0,1,2:T(8,128)S(1)} copy(f32[2048,8,8]{2,1,0:T(8,128)} %fusion.58) | data formatting | bytes 1048576 | tf_op jit(solution)/shard_map/hjf,hif->jif/dot_general | solution.py:50
  346.0 5.2 %copy.29 = f32[2048,8,8]{0,1,2:T(8,128)S(1)} copy(f32[2048,8,8]{2,1,0:T(8,128)} %fusion.60) | data formatting | bytes 1048576 | tf_op jit(solution)/shard_map/hjf,hif->jif/dot_general | solution.py:53
  351.2 5.2 %copy.28 = f32[2048,8,8]{0,1,2:T(8,128)S(1)} copy(f32[2048,8,8]{2,1,0:T(8,128)} %fusion.59) | data formatting | bytes 1048576 | tf_op jit(solution)/shard_map/hjf,hif->jif/dot_general | solution.py:53
  356.4 9.4 %fusion.9 = f32[8,8,512]{2,1,0:T(8,128)} fusion(f32[2048,512]{1,0:T(8,128)} %get-tuple-element.20, f32[2048,512]{1,0:T(8,128)} %get-tuple-element.19, f32[8,8,2048]{2,1,0:T(8,128)S(1)} %get-tuple-element.27, f32[8,8,2048]{2,1,0:T(8,128)S(1)} %get-tuple-element.28), kind=kOutput, calls=%fused_computation.13 | convolution fusion | flops 1615069184 | bytes 9568256 | tf_op jit(solution)/shard_map/dot_general | solution.py:62
  366.0 9.4 %fusion.7 = f32[8,8,512]{2,1,0:T(8,128)} fusion(f32[2048,512]{1,0:T(8,128)} %get-tuple-element.20, f32[2048,512]{1,0:T(8,128)} %get-tuple-element.19, f32[8,8,2048]{2,1,0:T(8,128)S(1)} %get-tuple-element.25, f32[8,8,2048]{2,1,0:T(8,128)S(1)} %get-tuple-element.26), kind=kOutput, calls=%fused_computation.12 | convolution fusion | flops 1615069184 | bytes 9568256 | tf_op jit(solution)/shard_map/dot_general | solution.py:62
  375.5 14.9 %reduce-scatter.9.cloned.1.call-done = f32[2,8,512]{2,1,0:T(8,128)} async-done(((f32[8,8,512]{2,1,0:T(8,128)}), f32[2,8,512]{2,1,0:T(8,128)}) %reduce-scatter.9.cloned.1.call-update) | async-done | bytes 32784 | tf_op jit(solution)/shard_map/reduce_scatter | solution.py:87
  390.4 26.7 %reduce-scatter.11.cloned.1.call-done = f32[2,8,512]{2,1,0:T(8,128)} async-done(((f32[8,8,512]{2,1,0:T(8,128)}), f32[2,8,512]{2,1,0:T(8,128)}) %reduce-scatter.11.cloned.1.call-update) | async-done | bytes 32784 | tf_op jit(solution)/shard_map/reduce_scatter | solution.py:87
  (97 shorter events, 31.6 us)
Async XLA Ops:
  6.5 2.8 copy-start.16
  6.5 2.8 copy-start.18
  6.5 368.9 %reduce-scatter.5.cloned.1.call-start = ((), (), s32[]{:S(2)}) async-start(), calls=%async_computation.4 | async-start | bytes 163840 | tf_op jit(solution)/shard_map/reduce_scatter | solution.py:87
  7.7 2.3 copy-start.17
  9.5 16.9 %collective-permute-start = (bf16[8,8,4096]{2,1,0:T(8,128)(2,1)S(1)}, bf16[8,8,4096]{2,1,0:T(8,128)(2,1)S(1)}, u32[]{:S(2)}, u32[]{:S(2)}) collective-permute-start(bf16[8,8,4096]{2,1,0:T(8,128)(2,1)S(1)} %fusion.17), channel_id=1, source_target_pairs={{0,4},{4,0},{8,12},{12,8},{16,20},{20,16},{24,28},{28,24},{1,5},{5... | collective-permute-start | bytes 1572872 | tf_op jit(solution)/shard_map/ppermute | solution.py:12
  26.5 22.8 %collective-permute-start.1 = (bf16[8,8,4096]{2,1,0:T(8,128)(2,1)S(1)}, bf16[8,8,4096]{2,1,0:T(8,128)(2,1)S(1)}, u32[]{:S(2)}, u32[]{:S(2)}) collective-permute-start(bf16[8,8,4096]{2,1,0:T(8,128)(2,1)S(1)} %get-tuple-element.5), channel_id=1, source_target_pairs={{0,8},{4,12},{8,0},{12,4},{16,24},{20,28},{24,16},{28,20},{1,9},{5... | collective-permute-start | bytes 1572872 | tf_op jit(solution)/shard_map/ppermute | solution.py:12
  47.1 26.0 %collective-permute-start.3 = (bf16[8,8,4096]{2,1,0:T(8,128)(2,1)S(1)}, bf16[8,8,4096]{2,1,0:T(8,128)(2,1)S(1)}, u32[]{:S(2)}, u32[]{:S(2)}) collective-permute-start(bf16[8,8,4096]{2,1,0:T(8,128)(2,1)S(1)} %get-tuple-element.8), channel_id=1, source_target_pairs={{0,8},{4,12},{8,0},{12,4},{16,24},{20,28},{24,16},{28,20},{1,9},{5... | collective-permute-start | bytes 1572872 | tf_op jit(solution)/shard_map/ppermute | solution.py:12
  47.3 47.4 %collective-permute-start.5 = (bf16[8,8,4096]{2,1,0:T(8,128)(2,1)S(1)}, bf16[8,8,4096]{2,1,0:T(8,128)(2,1)S(1)}, u32[]{:S(2)}, u32[]{:S(2)}) collective-permute-start(bf16[8,8,4096]{2,1,0:T(8,128)(2,1)S(1)} %get-tuple-element.7), channel_id=1, source_target_pairs={{0,8},{4,12},{8,0},{12,4},{16,24},{20,28},{24,16},{28,20},{1,9},{5... | collective-permute-start | bytes 1572872 | tf_op jit(solution)/shard_map/ppermute | solution.py:12
  49.1 56.0 %collective-permute-start.7 = (bf16[8,8,4096]{2,1,0:T(8,128)(2,1)S(1)}, bf16[8,8,4096]{2,1,0:T(8,128)(2,1)S(1)}, u32[]{:S(2)}, u32[]{:S(2)}) collective-permute-start(bf16[8,8,4096]{2,1,0:T(8,128)(2,1)S(1)} %get-tuple-element.6), channel_id=1, source_target_pairs={{0,8},{4,12},{8,0},{12,4},{16,24},{20,28},{24,16},{28,20},{1,9},{5... | collective-permute-start | bytes 1572872 | tf_op jit(solution)/shard_map/ppermute | solution.py:12
  49.3 56.0 %collective-permute-start.2 = (bf16[8,8,4096]{2,1,0:T(8,128)(2,1)S(1)}, bf16[8,8,4096]{2,1,0:T(8,128)(2,1)S(1)}, u32[]{:S(2)}, u32[]{:S(2)}) collective-permute-start(bf16[8,8,4096]{2,1,0:T(8,128)(2,1)S(1)} %broadcast_select_fusion.10), channel_id=1, source_target_pairs={{0,16},{4,20},{8,24},{12,28},{16,0},{20,4},{24,8},{28,12},{1,17},{... | collective-permute-start | bytes 1572872 | tf_op jit(solution)/shard_map/ppermute | solution.py:12
  73.2 66.6 %collective-permute-start.4 = (bf16[8,8,4096]{2,1,0:T(8,128)(2,1)S(1)}, bf16[8,8,4096]{2,1,0:T(8,128)(2,1)}, u32[]{:S(2)}, u32[]{:S(2)}) collective-permute-start(bf16[8,8,4096]{2,1,0:T(8,128)(2,1)S(1)} %broadcast_select_fusion.7), channel_id=1, source_target_pairs={{0,16},{4,20},{8,24},{12,28},{16,0},{20,4},{24,8},{28,12},{1,17},{... | collective-permute-start | bytes 1572872 | tf_op jit(solution)/shard_map/ppermute | solution.py:12
  94.7 82.8 %collective-permute-start.6 = (bf16[8,8,4096]{2,1,0:T(8,128)(2,1)S(1)}, bf16[8,8,4096]{2,1,0:T(8,128)(2,1)S(1)}, u32[]{:S(2)}, u32[]{:S(2)}) collective-permute-start(bf16[8,8,4096]{2,1,0:T(8,128)(2,1)S(1)} %broadcast_select_fusion.4), channel_id=1, source_target_pairs={{0,16},{4,20},{8,24},{12,28},{16,0},{20,4},{24,8},{28,12},{1,17},{... | collective-permute-start | bytes 1572872 | tf_op jit(solution)/shard_map/ppermute | solution.py:12
  105.2 110.2 %collective-permute-start.8 = (bf16[8,8,4096]{2,1,0:T(8,128)(2,1)S(1)}, bf16[8,8,4096]{2,1,0:T(8,128)(2,1)S(1)}, u32[]{:S(2)}, u32[]{:S(2)}) collective-permute-start(bf16[8,8,4096]{2,1,0:T(8,128)(2,1)S(1)} %broadcast_select_fusion.1), channel_id=1, source_target_pairs={{0,16},{4,20},{8,24},{12,28},{16,0},{20,4},{24,8},{28,12},{1,17},{... | collective-permute-start | bytes 1572872 | tf_op jit(solution)/shard_map/ppermute | solution.py:12
  113.9 9.2 %copy-start.4 = (bf16[8,8,2048]{0,1,2:T(8,128)(2,1)S(1)}, bf16[8,8,2048]{0,1,2:T(8,128)(2,1)}, u32[]{:S(2)}) copy-start(bf16[8,8,2048]{0,1,2:T(8,128)(2,1)} %copy.4) | copy-start | bytes 786436
  113.9 9.2 %copy-start.8 = (bf16[8,8,2048]{1,0,2:T(8,128)(2,1)S(1)}, bf16[8,8,2048]{1,0,2:T(8,128)(2,1)}, u32[]{:S(2)}) copy-start(bf16[8,8,2048]{1,0,2:T(8,128)(2,1)} %copy.5) | copy-start | bytes 786436
  123.1 5.6 %copy-start.9 = (bf16[8,8,2048]{1,0,2:T(8,128)(2,1)S(1)}, bf16[8,8,2048]{1,0,2:T(8,128)(2,1)}, u32[]{:S(2)}) copy-start(bf16[8,8,2048]{1,0,2:T(8,128)(2,1)} %copy.8) | copy-start | bytes 786436
  128.6 5.6 %copy-start = (bf16[8,8,2048]{0,1,2:T(8,128)(2,1)S(1)}, bf16[8,8,2048]{0,1,2:T(8,128)(2,1)}, u32[]{:S(2)}) copy-start(bf16[8,8,2048]{0,1,2:T(8,128)(2,1)} %copy.7) | copy-start | bytes 786436
  144.1 9.2 %copy-start.1 = (bf16[8,8,2048]{0,1,2:T(8,128)(2,1)S(1)}, bf16[8,8,2048]{0,1,2:T(8,128)(2,1)}, u32[]{:S(2)}) copy-start(bf16[8,8,2048]{0,1,2:T(8,128)(2,1)} %copy.7) | copy-start | bytes 786436
  144.1 9.2 %copy-start.11 = (bf16[8,8,2048]{1,0,2:T(8,128)(2,1)S(1)}, bf16[8,8,2048]{1,0,2:T(8,128)(2,1)}, u32[]{:S(2)}) copy-start(bf16[8,8,2048]{1,0,2:T(8,128)(2,1)} %copy.12) | copy-start | bytes 786436
  162.8 9.2 %copy-start.5 = (bf16[8,8,2048]{0,1,2:T(8,128)(2,1)S(1)}, bf16[8,8,2048]{0,1,2:T(8,128)(2,1)}, u32[]{:S(2)}) copy-start(bf16[8,8,2048]{0,1,2:T(8,128)(2,1)} %copy.4) | copy-start | bytes 786436
  162.8 9.2 %copy-start.12 = (bf16[8,8,2048]{1,0,2:T(8,128)(2,1)S(1)}, bf16[8,8,2048]{1,0,2:T(8,128)(2,1)}, u32[]{:S(2)}) copy-start(bf16[8,8,2048]{1,0,2:T(8,128)(2,1)} %copy.14) | copy-start | bytes 786436
  181.8 9.3 %copy-start.2 = (bf16[8,8,2048]{0,1,2:T(8,128)(2,1)S(1)}, bf16[8,8,2048]{0,1,2:T(8,128)(2,1)}, u32[]{:S(2)}) copy-start(bf16[8,8,2048]{0,1,2:T(8,128)(2,1)} %copy.7) | copy-start | bytes 786436
  181.8 9.3 %copy-start.13 = (bf16[8,8,2048]{1,0,2:T(8,128)(2,1)S(1)}, bf16[8,8,2048]{1,0,2:T(8,128)(2,1)}, u32[]{:S(2)}) copy-start(bf16[8,8,2048]{1,0,2:T(8,128)(2,1)} %copy.18) | copy-start | bytes 786436
  200.6 9.1 %copy-start.6 = (bf16[8,8,2048]{0,1,2:T(8,128)(2,1)S(1)}, bf16[8,8,2048]{0,1,2:T(8,128)(2,1)}, u32[]{:S(2)}) copy-start(bf16[8,8,2048]{0,1,2:T(8,128)(2,1)} %copy.4) | copy-start | bytes 786436
  200.6 9.1 %copy-start.14 = (bf16[8,8,2048]{1,0,2:T(8,128)(2,1)S(1)}, bf16[8,8,2048]{1,0,2:T(8,128)(2,1)}, u32[]{:S(2)}) copy-start(bf16[8,8,2048]{1,0,2:T(8,128)(2,1)} %copy.20) | copy-start | bytes 786436
  219.9 9.2 %copy-start.7 = (bf16[8,8,2048]{0,1,2:T(8,128)(2,1)S(1)}, bf16[8,8,2048]{0,1,2:T(8,128)(2,1)}, u32[]{:S(2)}) copy-start(bf16[8,8,2048]{0,1,2:T(8,128)(2,1)} %copy.4) | copy-start | bytes 786436
  220.0 9.2 %copy-start.15 = (bf16[8,8,2048]{1,0,2:T(8,128)(2,1)S(1)}, bf16[8,8,2048]{1,0,2:T(8,128)(2,1)}, u32[]{:S(2)}) copy-start(bf16[8,8,2048]{1,0,2:T(8,128)(2,1)} %copy.26) | copy-start | bytes 786436
  238.8 9.2 %copy-start.3 = (bf16[8,8,2048]{0,1,2:T(8,128)(2,1)S(1)}, bf16[8,8,2048]{0,1,2:T(8,128)(2,1)}, u32[]{:S(2)}) copy-start(bf16[8,8,2048]{0,1,2:T(8,128)(2,1)} %copy.7) | copy-start | bytes 786436
  238.8 9.2 %copy-start.10 = (bf16[8,8,2048]{1,0,2:T(8,128)(2,1)S(1)}, bf16[8,8,2048]{1,0,2:T(8,128)(2,1)}, u32[]{:S(2)}) copy-start(bf16[8,8,2048]{1,0,2:T(8,128)(2,1)} %copy.24) | copy-start | bytes 786436
  284.0 91.5 %reduce-scatter.7.cloned.1.call-start = ((), (), s32[]{:S(2)}) async-start(), calls=%async_computation.5 | async-start | bytes 163840 | tf_op jit(solution)/shard_map/reduce_scatter | solution.py:87
  335.2 55.2 %reduce-scatter.9.cloned.1.call-start = ((), (), s32[]{:S(2)}) async-start(), calls=%async_computation.6 | async-start | bytes 163840 | tf_op jit(solution)/shard_map/reduce_scatter | solution.py:87
  365.8 51.2 %reduce-scatter.11.cloned.1.call-start = ((), (), s32[]{:S(2)}) async-start(), calls=%async_computation.7 | async-start | bytes 163840 | tf_op jit(solution)/shard_map/reduce_scatter | solution.py:87
Sparse Core Ops, SparseCore 0:
  284.1 24.3 reduce-scatter.4
  335.3 24.3 reduce-scatter.6
  365.9 24.3 reduce-scatter.8
  393.2 23.8 reduce-scatter.10
where the time goes:
time: 431 us; the launch traced here: 425 us
  matrix products  152 us (35%)
  local copies, waits for them, and re-layouts  127 us (29%)
  waiting for transfers between devices  93.8 us (22%)
  other arithmetic  22.3 us (5%)
  between operations  21.4 us (5%)
  starting transfers between devices  9.2 us (2%)
    ppermute x9, waiting for transfers between devices, partner_2(): lax.ppermute(value, axis, [(i, i ^ 1 << apart) for i in range(lax.axis_si...  52.1 us
    reduce_scatter x4, waiting for transfers between devices, per_device(): lax.psum_scatter(term_rows(jnp.int32(0), lax.axis_size('hour') * (chans /...  41.6 us
    dot_general x4, matrix products, to_lags(): jnp.dot(flat, weights, precision=lax.Precision.HIGHEST, preferred_element...  37.5 us
    dot_general x4, matrix products, cross_spectrum(): jnp.einsum('hjf,hif->jif', far_re, own_re, preferred_element_type=f32)  33.2 us
    dot_general x4, matrix products, cross_spectrum(): jnp.einsum('hjf,hif->jif', far_im, own_im, preferred_element_type=f32)  33 us
    dot_general x4, matrix products, cross_spectrum(): jnp.einsum('hjf,hif->jif', far_re, own_im, preferred_element_type=f32)  25.8 us
    dot_general x4, matrix products, cross_spectrum(): jnp.einsum('hjf,hif->jif', far_im, own_re, preferred_element_type=f32)  22.4 us
    dot_general x4, local copies, waits for them, and re-layouts, cross_spectrum(): jnp.einsum('hjf,hif->jif', far_re, own_re, preferred_element_type=f32)  21 us
  transfers between devices with their start and end apart: 13, of which 5 were waited for; matrix products, arithmetic and copies ran while one was open for 54% of the time, Pallas kernels for 0%

commit v1 on v0

v1 whole, which is shorter than its diff:
```python
import functools

import jax
import jax.numpy as jnp
import ml_dtypes
import numpy as np
from jax import lax
from jax.experimental import pallas as pl
from jax.experimental.pallas import tpu as pltpu
from jax.sharding import PartitionSpec as P

BAND = 64
LAGS = 512
ROUNDS = 4
CHUNKS = 4
LANES = 128
MESH = pl.DeviceIdType.MESH
F32 = jnp.float32
BF16 = jnp.bfloat16


def lag_tables(n_freq, total_hours, chunks):
    lag = np.arange(LAGS, dtype=np.int64)[None, :] - LAGS // 2
    phase = np.arange(n_freq, dtype=np.int64)[:, None] * lag % (2 * n_freq)
    angle = np.pi * phase.astype(np.float64) / n_freq
    factor = 1.0 / np.sqrt(float(total_hours * n_freq))
    part = n_freq // chunks
    cos = (np.cos(angle) * factor).reshape(chunks, part, LAGS)
    sin = (-np.sin(angle) * factor).reshape(chunks, part, LAGS)
    table = np.concatenate([cos, sin], axis=1)
    high = table.astype(ml_dtypes.bfloat16)
    low = (table - high.astype(np.float64)).astype(ml_dtypes.bfloat16)
    return high, low


def split(value):
    high = value.astype(BF16)
    return high, (value - high.astype(F32)).astype(BF16)


def kernel(dims, plan_ref, spectra_ref, quality_ref, high_ref, low_ref, out_ref, *scratch):
    n_chan, n_hour, hours, chans, n_freq = dims
    held = scratch[:CHUNKS]
    (own, far, cross, total, arrived, high, low, table_sem,
     line_send, line_recv, twin_send, twin_recv, sum_send, sum_recv) = scratch[CHUNKS:]
    n_chip = n_chan // 2
    rows = hours * chans
    part = n_freq // CHUNKS
    per_hour = chans // n_hour
    share = ROUNDS * per_hour * chans
    me, my_hour = lax.axis_index("chan"), lax.axis_index("hour")
    chip, core = me // 2, me % 2
    twin = chip * 2 + 1 - core
    has = (chip < n_chip - 1, chip > 0)
    neighbour = (jnp.minimum(chip + 1, n_chip - 1) * 2 + core, jnp.maximum(chip - 1, 0) * 2 + core)

    loads = [pltpu.make_async_copy(high_ref, high, table_sem.at[0]),
             pltpu.make_async_copy(low_ref, low, table_sem.at[1])]
    for load in loads:
        load.start()

    barrier = pltpu.get_barrier_semaphore()
    pl.semaphore_signal(barrier, inc=1, device_id=(twin, my_hour), device_id_type=MESH)
    for way in range(2):
        @pl.when(has[way])
        def _(way=way):
            pl.semaphore_signal(barrier, inc=1, device_id=(neighbour[way], my_hour), device_id_type=MESH)
    for step in range(1, n_hour):
        pl.semaphore_signal(barrier, inc=1, device_id=(me, lax.rem(my_hour + step, n_hour)), device_id_type=MESH)

    half = lax.broadcasted_iota(jnp.int32, (LANES, LANES), 0) // BAND
    half_out = lax.broadcasted_iota(jnp.int32, (LANES, LANES), 1) // BAND
    ones = jnp.where(half == half_out, 1.0, 0.0).astype(BF16)
    quality = quality_ref[...]

    def whiten(chunk):
        def tile(at, carry):
            cols = pl.multiple_of(at * LANES, LANES)
            re_at = pl.multiple_of(chunk * part + cols, LANES)
            im_at = pl.multiple_of(n_freq + chunk * part + cols, LANES)
            re = spectra_ref[:, :, pl.ds(re_at, LANES)].astype(F32).reshape(rows, LANES)
            im = spectra_ref[:, :, pl.ds(im_at, LANES)].astype(F32).reshape(rows, LANES)
            power = re * re + im * im
            first, rest = power.astype(BF16), power
            rest = rest - first.astype(F32)
            second = rest.astype(BF16)
            third = (rest - second.astype(F32)).astype(BF16)
            band = jnp.dot(first, ones, preferred_element_type=F32)
            band += jnp.dot(second, ones, preferred_element_type=F32)
            band += jnp.dot(third, ones, preferred_element_type=F32)
            gain = lax.rsqrt(band * (1.0 / BAND) + 1e-6)
            re_out = (re * gain * quality).astype(BF16)
            im_out = (im * gain * quality).astype(BF16)
            im_cols = pl.multiple_of(part + cols, LANES)
            held[chunk][me, :, pl.ds(cols, LANES)] = re_out
            held[chunk][me, :, pl.ds(im_cols, LANES)] = im_out
            own[chunk, :, pl.ds(cols, LANES)] = re_out.astype(F32)
            own[chunk, :, pl.ds(im_cols, LANES)] = im_out.astype(F32)
            return carry

        lax.fori_loop(0, part // LANES, tile, 0)

    def line(chunk, step, way, block):
        slot = held[chunk].at[block * 2 + core]
        return pltpu.make_async_remote_copy(
            src_ref=slot, dst_ref=slot,
            send_sem=line_send.at[chunk, step, way], recv_sem=line_recv.at[chunk, step, way],
            device_id=(neighbour[way], my_hour), device_id_type=MESH)

    def to_twin(chunk, step, way, block, side):
        slot = held[chunk].at[block * 2 + side]
        return pltpu.make_async_remote_copy(
            src_ref=slot, dst_ref=slot,
            send_sem=twin_send.at[chunk, step, way], recv_sem=twin_recv.at[chunk, step, way],
            device_id=(twin, my_hour), device_id_type=MESH)

    def sends(step, way):
        block = chip - step if way == 0 else chip + step
        ok = block >= 0 if way == 0 else block <= n_chip - 1
        return jnp.clip(block, 0, n_chip - 1), jnp.logical_and(ok, has[way])

    def receives(step, way):
        block = chip - 1 - step if way == 0 else chip + 1 + step
        ok = block >= 0 if way == 0 else block <= n_chip - 1
        return jnp.clip(block, 0, n_chip - 1), ok

    def start_line(chunk, step, way):
        block, ok = sends(step, way)
        pl.when(ok)(lambda: line(chunk, step, way, block).start())

    whiten(0)
    pl.semaphore_wait(barrier, n_hour + (chip < n_chip - 1).astype(jnp.int32) + (chip > 0).astype(jnp.int32))

    for chunk in range(CHUNKS):
        if chunk:
            whiten(chunk)
        for way in range(2):
            start_line(chunk, 0, way)
        to_twin(chunk, 0, 0, chip, core).start()

    def pass_on(chunk, step):
        for way in range(2):
            block, ok = receives(step, way)

            @pl.when(ok)
            def _(way=way, block=block):
                line(chunk, step, way, block).wait_recv()
                if step + 1 < n_chip - 1:
                    start_line(chunk, step + 1, way)
                to_twin(chunk, step + 1, way, block, core).start()

    def work(chunk):
        to_twin(chunk, 0, 0, chip, 1 - core).wait_recv()
        for step in range(n_chip - 1):
            for way in range(2):
                block, ok = receives(step, way)
                pl.when(ok)(lambda: to_twin(chunk, step + 1, way, block, 1 - core).wait_recv())
        if chunk == 0:
            for load in loads:
                load.wait()
        for rnd in range(ROUNDS):
            partner = jnp.bitwise_xor(me, plan_ref[rnd])
            far[rnd] = held[chunk][partner].astype(F32)

        def tile(at, carry):
            rnd, cols = at // (part // LANES), at % (part // LANES) * LANES
            re_at = pl.ds(pl.multiple_of(cols, LANES), LANES)
            im_at = pl.ds(pl.multiple_of(part + cols, LANES), LANES)
            sums_re = [jnp.zeros((chans, LANES), F32)] * chans
            sums_im = [jnp.zeros((chans, LANES), F32)] * chans
            for hour in range(hours):
                own_re = own[chunk, hour * chans:(hour + 1) * chans, re_at]
                own_im = own[chunk, hour * chans:(hour + 1) * chans, im_at]
                for j in range(chans):
                    far_re = far[rnd, hour * chans + j:hour * chans + j + 1, re_at]
                    far_im = far[rnd, hour * chans + j:hour * chans + j + 1, im_at]
                    sums_re[j] += own_re * far_re + own_im * far_im
                    sums_im[j] += own_im * far_re - own_re * far_im
            for j in range(chans):
                start = (j // per_hour) * share + (rnd * per_hour + j % per_hour) * chans
                at_rows = pl.ds(pl.multiple_of(start, 8), chans)
                cross[at_rows, re_at] = sums_re[j]
                cross[at_rows, im_at] = sums_im[j]
            return carry

        lax.fori_loop(0, ROUNDS * (part // LANES), tile, 0)

        first, second = split(cross[...])
        lagged = jnp.dot(first, high[chunk], preferred_element_type=F32)
        lagged += jnp.dot(second, high[chunk], preferred_element_type=F32)
        lagged += jnp.dot(first, low[chunk], preferred_element_type=F32)
        if chunk == 0:
            total[...] = lagged
        else:
            total[...] += lagged

    for step in range(n_chip - 2):
        for chunk in range(CHUNKS):
            pass_on(chunk, step)
    for chunk in range(CHUNKS):
        pass_on(chunk, n_chip - 2)
        if chunk:
            work(chunk - 1)
    work(CHUNKS - 1)

    def give(step):
        goal = lax.rem(my_hour + step, n_hour)
        return pltpu.make_async_remote_copy(
            src_ref=total.at[pl.ds(pl.multiple_of(goal * share, 8), share)],
            dst_ref=arrived.at[step - 1],
            send_sem=sum_send.at[step - 1], recv_sem=sum_recv.at[step - 1],
            device_id=(me, goal), device_id_type=MESH)

    for step in range(1, n_hour):
        give(step).start()

    for chunk in range(CHUNKS):
        to_twin(chunk, 0, 0, chip, core).wait_send()
        for step in range(n_chip - 1):
            for way in range(2):
                block, ok = sends(step, way)
                pl.when(ok)(lambda: line(chunk, step, way, block).wait_send())
                block, ok = receives(step, way)
                pl.when(ok)(lambda: to_twin(chunk, step + 1, way, block, core).wait_send())

    result = total[pl.ds(pl.multiple_of(my_hour * share, 8), share), :]
    for step in range(1, n_hour):
        give(step).wait_recv()
        result += arrived[step - 1]
    out_ref[...] = result.reshape(ROUNDS, per_hour, chans, LAGS)
    for step in range(1, n_hour):
        give(step).wait_send()


def per_device(spectra, quality, plan):
    hours, chans, width = spectra.shape
    n_freq = width // 2
    n_chan, n_hour = lax.axis_size("chan"), lax.axis_size("hour")
    n_chip = n_chan // 2
    rows = hours * chans
    part = n_freq // CHUNKS
    per_hour = chans // n_hour
    share = ROUNDS * per_hour * chans
    high, low = lag_tables(n_freq, hours * n_hour, CHUNKS)
    by_row = jnp.broadcast_to(
        jnp.tile(quality.astype(F32), hours)[:, None], (rows, LANES))
    vmem = pl.BlockSpec(memory_space=pltpu.VMEM)
    dma = pltpu.SemaphoreType.DMA
    return pl.pallas_call(
        functools.partial(kernel, (n_chan, n_hour, hours, chans, n_freq)),
        out_shape=jax.ShapeDtypeStruct((ROUNDS, per_hour, chans, LAGS), F32),
        in_specs=[pl.BlockSpec(memory_space=pltpu.SMEM), vmem, vmem,
                  pl.BlockSpec(memory_space=pl.ANY), pl.BlockSpec(memory_space=pl.ANY)],
        out_specs=vmem,
        scratch_shapes=[pltpu.VMEM((n_chan, rows, 2 * part), BF16)] * CHUNKS + [
            pltpu.VMEM((CHUNKS, rows, 2 * part), F32),
            pltpu.VMEM((ROUNDS, rows, 2 * part), F32),
            pltpu.VMEM((n_hour * share, 2 * part), F32),
            pltpu.VMEM((n_hour * share, LAGS), F32),
            pltpu.VMEM((n_hour - 1, share, LAGS), F32),
            pltpu.VMEM(high.shape, BF16),
            pltpu.VMEM(low.shape, BF16),
            dma((2,)),
            dma((CHUNKS, n_chip - 1, 2)),
            dma((CHUNKS, n_chip - 1, 2)),
            dma((CHUNKS, n_chip, 2)),
            dma((CHUNKS, n_chip, 2)),
            dma((n_hour - 1,)),
            dma((n_hour - 1,)),
        ],
        compiler_params=pltpu.CompilerParams(
            collective_id=0, has_side_effects=True, vmem_limit_bytes=48 * 1024 * 1024),
    )(plan, spectra, by_row, jnp.asarray(high), jnp.asarray(low))


def solution(mesh):
    return jax.shard_map(
        per_device,
        mesh=mesh,
        in_specs=(P("hour", "chan", None), P("chan"), P()),
        out_specs=P(None, "hour", "chan", None),
        check_vma=False,
    )
```

time: 431 us -> 58.5 us (0.14); the launches traced: 425 us -> 58.3 us
  matrix products: 152 us -> 0 us
  local copies, waits for them, and re-layouts: 127 us -> 4.71 us
  waiting for transfers between devices: 93.8 us -> 0 us
  Pallas kernels: 0 us -> 52.9 us
  other arithmetic: 22.3 us -> 0.66 us
  between operations: 21.4 us -> 0.01 us
  starting transfers between devices: 9.2 us -> 0 us
    dot_general x20 -> x0, matrix products: 152 us -> none  [the longest x4 37.5 us: to_lags(): jnp.dot(flat, weights, precision=lax.Precision.HIGHEST, preferred_element...]
    dot_general x16 -> x0, local copies, waits for them, and re-layouts: 83.4 us -> none  [the longest x4 21 us: cross_spectrum(): jnp.einsum('hjf,hif->jif', far_re, own_re, preferred_element_type=f32)]
    pallas_call x0 -> x1, Pallas kernels: none -> 52.9 us  [per_device(): pl.pallas_call(functools.partial(kernel, (n_chan, n_hour, hours, chans, n...]
    ppermute x9 -> x0, waiting for transfers between devices: 52.1 us -> none  [partner_2(): lax.ppermute(value, axis, [(i, i ^ 1 << apart) for i in range(lax.axis_si...]
    slice x16 -> x0, local copies, waits for them, and re-layouts: 42.1 us -> none  [the longest x8 16.8 us: cross_spectrum(): far_im = partner[..., n_freq:]]
    reduce_scatter x4 -> x0, waiting for transfers between devices: 41.6 us -> none  [per_device(): lax.psum_scatter(term_rows(jnp.int32(0), lax.axis_size('hour') * (chans /...]
    cos x1 -> x0, other arithmetic: 17.9 us -> none  [lag_table(): return jnp.concatenate([jnp.cos(angle), -jnp.sin(angle)], axis=0) * factor]
    ppermute x9 -> x0, starting transfers between devices: 9.07 us -> none  [partner_2(): lax.ppermute(value, axis, [(i, i ^ 1 << apart) for i in range(lax.axis_si...]
  transfers between devices with their start and end apart: 13 -> 0, of which waited for: 5 -> 0; matrix products, arithmetic and copies ran while one was open for 54% -> 0% of each run, Pallas kernels for 0% -> 0%
where the time goes in v1:
time: 58.5 us; the launch traced here: 58.3 us
  Pallas kernels  52.9 us (90%)
  local copies, waits for them, and re-layouts  4.71 us (8%)
  other arithmetic  0.66 us (1%)
    pallas_call x1, Pallas kernels, per_device(): pl.pallas_call(functools.partial(kernel, (n_chan, n_hour, hours, chans, n...  52.9 us
    unnamed x7, local copies, waits for them, and re-layouts  4.55 us

profile of v1, /device:TPU:0, one launch (start us, length us, event | category | flops | bytes accessed | tf_op | source)
XLA Modules:
  0.0 58.3 jit_solution(8710709161813575497)
XLA Ops:
  0.0 0.7 %convert_element_type.3 = f32[8]{0:T(128)S(1)} convert(s32[8]{0:T(128)} %param.6) | non-fusion elementwise | flops 8 | bytes 64 | tf_op jit(solution)/shard_map/convert_element_type | solution.py:246
  0.7 0.1 broadcast_in_dim.7
  0.7 0.1 broadcast_in_dim.8.quality_ref
  0.8 0.0 copy-start
  0.8 2.2 %copy-done = bf16[4,1024,512]{2,1,0:T(8,128)(2,1)S(1)} copy-done((bf16[4,1024,512]{2,1,0:T(8,128)(2,1)S(1)}, bf16[4,1024,512]{2,1,0:T(8,128)(2,1)}, u32[]{:S(2)}) %copy-start) | copy-done | bytes 4194328
  3.0 0.0 copy-start.1
  3.0 1.0 %copy-done.1 = bf16[8,8,4096]{2,1,0:T(8,128)(2,1)S(1)} copy-done((bf16[8,8,4096]{2,1,0:T(8,128)(2,1)S(1)}, bf16[8,8,4096]{2,1,0:T(8,128)(2,1)}, u32[]{:S(2)}) %copy-start.1) | copy-done | bytes 524312
  4.1 0.0 copy-start.2
  4.1 0.7 %copy-done.2 = s32[4]{0:T(128)S(1)} copy-done((s32[4]{0:T(128)S(1)}, s32[4]{0:T(128)}, u32[]{:S(2)}) %copy-start.2) | copy-done | bytes 40
  4.7 52.9 %shard_map.55 = f32[4,2,8,512]{3,2,1,0:T(8,128)S(1)} custom-call(s32[4]{0:T(128)S(1)} %copy-done.2, bf16[8,8,4096]{2,1,0:T(8,128)(2,1)S(1)} %copy-done.1, f32[64,128]{1,0:T(8,128)S(1)} %broadcast_in_dim.8.quality_ref, bf16[4,1024,512]{2,1,0:T(8,128)(2,1)S(1)} %copy-done, bf16[4,1024,512]{2,1,0:T(8,128)(2,1)} %constant.5.clone.low_ref), custom_call_target="tpu_custom_call" | custom-call | tf_op jit(solution)/shard_map/pallas_call | solution.py:249
  57.7 0.7 %copy.7 = f32[4,2,8,512]{3,2,1,0:T(8,128)} copy(f32[4,2,8,512]{3,2,1,0:T(8,128)S(1)} %shard_map.55) | data formatting | bytes 262144
  (1 shorter events, 0.0 us)
Async XLA Ops:
  0.8 2.2 %copy-start = (bf16[4,1024,512]{2,1,0:T(8,128)(2,1)S(1)}, bf16[4,1024,512]{2,1,0:T(8,128)(2,1)}, u32[]{:S(2)}) copy-start(bf16[4,1024,512]{2,1,0:T(8,128)(2,1)} %constant.4.clone.high_ref) | copy-start | bytes 12582916
  3.0 1.0 %copy-start.1 = (bf16[8,8,4096]{2,1,0:T(8,128)(2,1)S(1)}, bf16[8,8,4096]{2,1,0:T(8,128)(2,1)}, u32[]{:S(2)}) copy-start(bf16[8,8,4096]{2,1,0:T(8,128)(2,1)} %spectra_ref.1) | copy-start | bytes 1572868
  4.1 0.7 %copy-start.2 = (s32[4]{0:T(128)S(1)}, s32[4]{0:T(128)}, u32[]{:S(2)}) copy-start(s32[4]{0:T(128)} %plan_ref.1) | copy-start | bytes 52

commit v2 on v1

--- a/solution.py
+++ b/solution.py
@@ -12,7 +12,7 @@
 BAND = 64
 LAGS = 512
 ROUNDS = 4
-CHUNKS = 4
+CHUNKS = 8
 LANES = 128
 MESH = pl.DeviceIdType.MESH
 F32 = jnp.float32
@@ -38,10 +38,10 @@
     return high, (value - high.astype(F32)).astype(BF16)
 
 
-def kernel(dims, plan_ref, spectra_ref, quality_ref, high_ref, low_ref, out_ref, *scratch):
+def kernel(dims, plan_ref, spectra_hbm, quality_ref, high_ref, low_ref, out_ref, *scratch):
     n_chan, n_hour, hours, chans, n_freq = dims
     held = scratch[:CHUNKS]
-    (own, far, cross, total, arrived, high, low, table_sem,
+    (own, far, cross, total, arrived, rounded, raw, high, low, table_sem,
      line_send, line_recv, twin_send, twin_recv, sum_send, sum_recv) = scratch[CHUNKS:]
     n_chip = n_chan // 2
     rows = hours * chans
@@ -54,6 +54,8 @@
     has = (chip < n_chip - 1, chip > 0)
     neighbour = (jnp.minimum(chip + 1, n_chip - 1) * 2 + core, jnp.maximum(chip - 1, 0) * 2 + core)
 
+    fetch = pltpu.make_async_copy(spectra_hbm, raw, table_sem.at[2])
+    fetch.start()
     loads = [pltpu.make_async_copy(high_ref, high, table_sem.at[0]),
              pltpu.make_async_copy(low_ref, low, table_sem.at[1])]
     for load in loads:
@@ -71,15 +73,19 @@
     half = lax.broadcasted_iota(jnp.int32, (LANES, LANES), 0) // BAND
     half_out = lax.broadcasted_iota(jnp.int32, (LANES, LANES), 1) // BAND
     ones = jnp.where(half == half_out, 1.0, 0.0).astype(BF16)
-    quality = quality_ref[...]
+    channel = lax.broadcasted_iota(jnp.int32, (chans, LANES), 0)
+    quality = jnp.zeros((chans, LANES), F32)
+    for c in range(chans):
+        quality = jnp.where(channel == c, quality_ref[c].astype(F32), quality)
+    quality = jnp.broadcast_to(quality[None], (hours, chans, LANES)).reshape(rows, LANES)
 
     def whiten(chunk):
         def tile(at, carry):
             cols = pl.multiple_of(at * LANES, LANES)
             re_at = pl.multiple_of(chunk * part + cols, LANES)
             im_at = pl.multiple_of(n_freq + chunk * part + cols, LANES)
-            re = spectra_ref[:, :, pl.ds(re_at, LANES)].astype(F32).reshape(rows, LANES)
-            im = spectra_ref[:, :, pl.ds(im_at, LANES)].astype(F32).reshape(rows, LANES)
+            re = raw[:, :, pl.ds(re_at, LANES)].astype(F32).reshape(rows, LANES)
+            im = raw[:, :, pl.ds(im_at, LANES)].astype(F32).reshape(rows, LANES)
             power = re * re + im * im
             first, rest = power.astype(BF16), power
             rest = rest - first.astype(F32)
@@ -128,6 +134,7 @@
         block, ok = sends(step, way)
         pl.when(ok)(lambda: line(chunk, step, way, block).start())
 
+    fetch.wait()
     whiten(0)
     pl.semaphore_wait(barrier, n_hour + (chip < n_chip - 1).astype(jnp.int32) + (chip > 0).astype(jnp.int32))
 
@@ -206,11 +213,12 @@
     def give(step):
         goal = lax.rem(my_hour + step, n_hour)
         return pltpu.make_async_remote_copy(
-            src_ref=total.at[pl.ds(pl.multiple_of(goal * share, 8), share)],
+            src_ref=rounded.at[pl.ds(pl.multiple_of(goal * share, 8), share)],
             dst_ref=arrived.at[step - 1],
             send_sem=sum_send.at[step - 1], recv_sem=sum_recv.at[step - 1],
             device_id=(me, goal), device_id_type=MESH)
 
+    rounded[...] = total[...].astype(BF16)
     for step in range(1, n_hour):
         give(step).start()
 
@@ -226,7 +234,7 @@
     result = total[pl.ds(pl.multiple_of(my_hour * share, 8), share), :]
     for step in range(1, n_hour):
         give(step).wait_recv()
-        result += arrived[step - 1]
+        result += arrived[step - 1].astype(F32)
     out_ref[...] = result.reshape(ROUNDS, per_hour, chans, LAGS)
     for step in range(1, n_hour):
         give(step).wait_send()
@@ -242,25 +250,24 @@
     per_hour = chans // n_hour
     share = ROUNDS * per_hour * chans
     high, low = lag_tables(n_freq, hours * n_hour, CHUNKS)
-    by_row = jnp.broadcast_to(
-        jnp.tile(quality.astype(F32), hours)[:, None], (rows, LANES))
-    vmem = pl.BlockSpec(memory_space=pltpu.VMEM)
+    smem, vmem, hbm = (pl.BlockSpec(memory_space=m) for m in (pltpu.SMEM, pltpu.VMEM, pltpu.HBM))
     dma = pltpu.SemaphoreType.DMA
     return pl.pallas_call(
         functools.partial(kernel, (n_chan, n_hour, hours, chans, n_freq)),
         out_shape=jax.ShapeDtypeStruct((ROUNDS, per_hour, chans, LAGS), F32),
-        in_specs=[pl.BlockSpec(memory_space=pltpu.SMEM), vmem, vmem,
-                  pl.BlockSpec(memory_space=pl.ANY), pl.BlockSpec(memory_space=pl.ANY)],
+        in_specs=[smem, hbm, smem, hbm, hbm],
         out_specs=vmem,
         scratch_shapes=[pltpu.VMEM((n_chan, rows, 2 * part), BF16)] * CHUNKS + [
             pltpu.VMEM((CHUNKS, rows, 2 * part), F32),
             pltpu.VMEM((ROUNDS, rows, 2 * part), F32),
             pltpu.VMEM((n_hour * share, 2 * part), F32),
             pltpu.VMEM((n_hour * share, LAGS), F32),
-            pltpu.VMEM((n_hour - 1, share, LAGS), F32),
+            pltpu.VMEM((n_hour - 1, share, LAGS), BF16),
+            pltpu.VMEM((n_hour * share, LAGS), BF16),
+            pltpu.VMEM(spectra.shape, BF16),
             pltpu.VMEM(high.shape, BF16),
             pltpu.VMEM(low.shape, BF16),
-            dma((2,)),
+            dma((3,)),
             dma((CHUNKS, n_chip - 1, 2)),
             dma((CHUNKS, n_chip - 1, 2)),
             dma((CHUNKS, n_chip, 2)),
@@ -269,8 +276,8 @@
             dma((n_hour - 1,)),
         ],
         compiler_params=pltpu.CompilerParams(
-            collective_id=0, has_side_effects=True, vmem_limit_bytes=48 * 1024 * 1024),
-    )(plan, spectra, by_row, jnp.asarray(high), jnp.asarray(low))
+            collective_id=0, has_side_effects=True, vmem_limit_bytes=63 * 1024 * 1024 + 960 * 1024),
+    )(plan, spectra, quality, jnp.asarray(high), jnp.asarray(low))
 
 
 def solution(mesh):

time: 58.5 us -> 52.4 us (0.90)
  local copies, waits for them, and re-layouts: 4.71 us -> 1.57 us
  Pallas kernels: 52.9 us -> 50.6 us
  other arithmetic: 0.66 us -> 0 us
    unnamed x7 -> x1, local copies, waits for them, and re-layouts: 4.55 us -> 1.57 us
    pallas_call x1, Pallas kernels: 52.9 us -> 50.6 us  [per_device(): pl.pallas_call(functools.partial(kernel, (n_chan, n_hour, hours, chans, n...]
    convert_element_type x1 -> x0, other arithmetic: 0.66 us -> none  [per_device(): quality.astype(F32)]
where the time goes in v2:
time: 52.4 us; the launch traced here: 52.2 us
  Pallas kernels  50.6 us (97%)
  local copies, waits for them, and re-layouts  1.57 us (3%)
    pallas_call x1, Pallas kernels, per_device(): pl.pallas_call(functools.partial(kernel, (n_chan, n_hour, hours, chans, n...  50.6 us
    unnamed x1, local copies, waits for them, and re-layouts  1.57 us

profile of v2, /device:TPU:0, one launch (start us, length us, event | category | flops | bytes accessed | tf_op | source)
XLA Modules:
  0.0 52.2 jit_solution(520686934636725465)
XLA Ops:
  0.0 50.6 %shard_map.55 = f32[4,2,8,512]{3,2,1,0:T(8,128)} custom-call(s32[4]{0:T(128)} %plan_ref.1, bf16[8,8,4096]{2,1,0:T(8,128)(2,1)} %spectra_hbm.1, s32[8]{0:T(128)} %quality_ref.1, bf16[8,512,512]{2,1,0:T(8,128)(2,1)} %constant.4.clone.high_ref, bf16[8,512,512]{2,1,0:T(8,128)(2,1)} %constant.5.clone.low_ref), custom_call_target="tpu_custom_call" | custom-call | tf_op jit(solution)/shard_map/pallas_call | solution.py:255
  50.6 1.6 %copy.7 = f32[4,2,8,512]{3,2,1,0:T(8,128)} copy(f32[4,2,8,512]{3,2,1,0:T(8,128)} %shard_map.55) | data formatting | bytes 262144
